TPU v7x, 128 devices: a whole 4x4x4 slice. The times are simulated.
128 devices in a mesh: dp: 32 (over z, x, y_lo), blk: 4 (over y_hi, core).
Axes of the slice: x: 4, y: 4 (y_hi: 2, y_lo: 2; y = y_hi * 2 + y_lo), z: 4, core: 2. Of those that a mesh axis runs over, the one named last changes fastest.
Arguments:
- hidden: bfloat16 [32, 1536, 768], P('dp', 'blk'), may hold values from -6 to 6
- output_grad: bfloat16 [32, 1536, 768], P('dp', 'blk'), may hold values from -6 to 6
- block_counts: int32 [32], P('dp'), may hold values from 2 to 3, as said below
- slot_table: int32 [32, 3], P('dp'), may hold values from 0 to 2, as said below
- block_order_two: int32 [12, 2], replicated, may hold values from 0 to 1, each once within a row
- block_order_three: int32 [12, 3], replicated, may hold values from 0 to 2, each once within a row
- query_weight: bfloat16 [2, 768, 768], replicated, may hold values from -0.21875 to 0.21875
- key_weight: bfloat16 [2, 768, 768], replicated, may hold values from -0.21875 to 0.21875
- value_weight: bfloat16 [2, 768, 768], replicated, may hold values from -0.21875 to 0.21875
- output_weight: bfloat16 [2, 768, 768], replicated, may hold values from -3.5 to 3.5
- query_bias: bfloat16 [2, 768], replicated, may hold values from -2 to 2
- value_bias: bfloat16 [2, 768], replicated, may hold values from -2 to 2
- output_bias: bfloat16 [2, 768], replicated, may hold values from -2 to 2
- expand_weight: bfloat16 [2, 768, 3072], replicated, may hold values from -0.21875 to 0.21875
- expand_bias: bfloat16 [2, 3072], replicated, may hold values from -2 to 2
- reduce_weight: bfloat16 [2, 3072, 768], replicated, may hold values from -0.109375 to 0.109375
- reduce_bias: bfloat16 [2, 768], replicated, may hold values from -2 to 2
- first_gain: bfloat16 [2, 768], replicated, may hold values from 0.5 to 1.5
- first_shift: bfloat16 [2, 768], replicated, may hold values from -2 to 2
- second_gain: bfloat16 [2, 768], replicated, may hold values from 0.5 to 1.5
- second_shift: bfloat16 [2, 768], replicated, may hold values from -2 to 2
Outputs:
- activations: bfloat16 [32, 1536, 768], P('dp', 'blk')
- input_grad: bfloat16 [32, 1536, 768], P('dp', 'blk')
- grad_query_weight: float32 [2, 768, 768], P(None, ('dp', 'blk'))
- grad_key_weight: float32 [2, 768, 768], P(None, ('dp', 'blk'))
- grad_value_weight: float32 [2, 768, 768], P(None, ('dp', 'blk'))
- grad_output_weight: float32 [2, 768, 768], P(None, ('dp', 'blk'))
- grad_query_bias: float32 [2, 768], P(None, ('dp', 'blk'))
- grad_value_bias: float32 [2, 768], P(None, ('dp', 'blk'))
- grad_output_bias: float32 [2, 768], P(None, ('dp', 'blk'))
- grad_expand_weight: float32 [2, 768, 3072], P(None, ('dp', 'blk'))
- grad_expand_bias: float32 [2, 3072], P(None, ('dp', 'blk'))
- grad_reduce_weight: float32 [2, 3072, 768], P(None, ('dp', 'blk'))
- grad_reduce_bias: float32 [2, 768], P(None, ('dp', 'blk'))
- grad_first_gain: float32 [2, 768], P(None, ('dp', 'blk'))
- grad_first_shift: float32 [2, 768], P(None, ('dp', 'blk'))
- grad_second_gain: float32 [2, 768], P(None, ('dp', 'blk'))
- grad_second_shift: float32 [2, 768], P(None, ('dp', 'blk'))
Inputs may be any that keep to these rules, and one draw needn't show every extreme that they name: `block_counts`: blocks of each sequence; its remaining slots are padding. Each row is a permutation: slot_table[s, j] is the slot of block j of sequence s; where block_counts[s] = 2, block 2 sits in slot 1. `block_order_two`: each row is a permutation. `block_order_three`: each row is a permutation.
All inputs are finite; a program needn't handle non-finite values.
Results may differ from a plain program's by a relative error of at most 0.03.
Values may be sent and summed in bfloat16 or wider, within the bound.
A program may use at most 320 MiB of HBM per device.

v0:
```python
import jax
import jax.numpy as jnp
from jax import lax
from jax.sharding import Mesh
from jax.sharding import PartitionSpec as P

D = 768
HEADS = 12
HD = 64
BLOCK = 512
SLOTS = 3
BLK = ("blk_0", "blk_1")
DP_BLK = ("dp_0", "dp_1", "dp_2", "blk_0", "blk_1")
DP = ("dp_0", "dp_1", "dp_2")


EPSILON = 1e-06
ROOT_HALF = 0.7071067811865476
INV_ROOT_TAU = 0.3989422804014327


def with_halo(array, sides, width):
    for axis, dim in sides:
        size, length = (lax.axis_size(axis), array.shape[dim])
        up = [(i, (i + 1) % size) for i in range(size - 1)]
        down = [(j, i) for i, j in up]
        last = lax.slice_in_dim(array, length - width, length, axis=dim)
        leading = lax.slice_in_dim(array, 0, width, axis=dim)
        before = lax.ppermute(last, axis, up)
        after = lax.ppermute(leading, axis, down)
        array = jnp.concatenate([before, array, after], axis=dim)
    return array


def from_behind(block, axis, distance):
    devices = range(lax.axis_size(axis))
    route = [(i - distance, i) for i in devices if i - distance in devices]
    return lax.ppermute(block, axis, route)


def side_by_side(arrays, axis, dim, along):
    widths = [a.shape[along] for a in arrays]
    both = jnp.concatenate(arrays, axis=along)
    filled = lax.all_gather(both, axis, axis=dim, tiled=True)
    return tuple(jnp.split(filled, [sum(widths[:k]) for k in range(1, len(widths))], axis=along))


def split_up(array, dim, size):
    shape = array.shape
    pieces = array.reshape(*shape[:dim], size, shape[dim] // size, *shape[dim + 1 :])
    return jnp.moveaxis(pieces, dim, 0)


def summed_rows(array, chips, core, dim):
    sizes = (lax.axis_size(chips), lax.axis_size(core))
    pieces = split_up(array, dim, sizes[0] * sizes[1])
    inside = pieces.shape[1:]
    pieces = pieces.reshape(*sizes, *inside).swapaxes(0, 1).reshape(-1, *inside)
    pieces = lax.psum_scatter(pieces, core, scatter_dimension=0, tiled=True)
    return lax.psum_scatter(pieces, chips, scatter_dimension=0, tiled=True)[0]


def side_by_side_2(arrays, axis, dim, along):
    ends, at = ([], 0)
    for a in arrays[:-1]:
        at += a.shape[along]
        ends.append(at)
    both = jnp.concatenate(arrays, axis=along)
    return tuple(
        jnp.split(lax.psum_scatter(both, axis, scatter_dimension=dim, tiled=True), ends, axis=along)
    )


def matmul(left, right):
    return jnp.dot(left, right, preferred_element_type=jnp.float32)


def contract_rows(left, right):
    return lax.dot_general(
        left, right, (((0,), (0,)), ((), ())), preferred_element_type=jnp.float32
    )


def times_transpose(left, right):
    return lax.dot_general(
        left, right, (((1,), (1,)), ((), ())), preferred_element_type=jnp.float32
    )


def norm_forward(residual, norm_gain, norm_shift):
    row_mean = jnp.mean(residual, axis=-1, keepdims=True)
    centred = residual - row_mean
    row_variance = jnp.mean(centred * centred, axis=-1, keepdims=True)
    inv_std = lax.rsqrt(row_variance + EPSILON)
    normed = centred * inv_std
    return (normed * norm_gain + norm_shift, normed, inv_std)


def norm_backward(grad_out, norm_gain, normed, inv_std):
    scaled = grad_out * norm_gain
    grad_input = inv_std * (
        scaled
        - jnp.mean(scaled, axis=-1, keepdims=True)
        - normed * jnp.mean(scaled * normed, axis=-1, keepdims=True)
    )
    return (grad_input, jnp.sum(grad_out * normed, axis=0), jnp.sum(grad_out, axis=0))


def gelu_slope(inner_pre):
    return 0.5 * (1.0 + lax.erf(inner_pre * ROOT_HALF)) + inner_pre * INV_ROOT_TAU * jnp.exp(
        -0.5 * inner_pre * inner_pre
    )


def live_pieces(slot_table, block_counts, piece_slot):
    positions = jnp.arange(SLOTS, dtype=jnp.int32)
    inverse = jnp.sum(
        positions[None, None, :] * (slot_table[:, None, :] == positions[None, :, None]), axis=2
    )
    block_number = jnp.sum(
        inverse[:, None, :] * (piece_slot[None, :, None] == positions[None, None, :]), axis=2
    )
    return (block_number, (block_number < block_counts[:, None]).astype(jnp.bfloat16))


def selection(slot_table, block_counts, order_two, order_three, block_number, swapped):
    positions = jnp.arange(SLOTS, dtype=jnp.int32)
    own_block = jnp.broadcast_to(block_number[:, :, None], block_number.shape + (HEADS,))
    if swapped:
        from_three = jnp.sum(
            (block_number[:, :, None, None] == positions[None, None, None, :])
            * order_three[None, None, :, :],
            axis=3,
        )
        pairs = jnp.arange(2, dtype=jnp.int32)
        from_two = jnp.sum(
            (jnp.minimum(block_number, 1)[:, :, None, None] == pairs[None, None, None, :])
            * order_two[None, None, :, :],
            axis=3,
        )
        chosen = jnp.where(
            block_counts[:, None, None] == SLOTS,
            from_three,
            jnp.where(own_block < 2, from_two, own_block),
        )
    else:
        chosen = own_block
    target = jnp.sum(
        (chosen[:, :, :, None] == positions[None, None, None, :]) * slot_table[:, None, None, :],
        axis=3,
    )
    return (target[:, :, :, None] == positions[None, None, None, :]).astype(jnp.bfloat16)


def pick_slots(picker, gathered):
    shaped = gathered.reshape(gathered.shape[0], SLOTS, BLOCK, HEADS, HD)
    return jnp.einsum(
        "spht,stkhd->sphkd", picker, shaped, preferred_element_type=jnp.float32
    ).astype(jnp.bfloat16)


def place_rims(widened, piece):
    seq_count = widened.shape[1]
    total_rows = piece * lax.axis_size(BLK)
    empty = jnp.zeros((2, seq_count, total_rows + 2 * piece, widened.shape[3]), widened.dtype)
    placed = lax.dynamic_update_slice_in_dim(empty, widened, lax.axis_index(BLK) * piece, 2)
    inside = placed[:, :, piece : piece + total_rows]
    return (inside[0], inside[1])


def neighbour_rows(key_local, value_local):
    piece = key_local.shape[1]
    stacked = jnp.stack([key_local, value_local])
    widened = with_halo(stacked, ((BLK, 2),), piece)
    return place_rims(widened, piece)


def return_rims(grad_keys, grad_values, piece):
    stacked = jnp.stack([grad_keys, grad_values])
    padded = jnp.pad(stacked, ((0, 0), (0, 0), (piece, piece), (0, 0)))
    window = lax.dynamic_slice_in_dim(padded, lax.axis_index(BLK) * piece, 3 * piece, 2)
    own_part = window[:, :, piece : 2 * piece]
    from_below = from_behind(window[:, :, 2 * piece :].astype(jnp.bfloat16), BLK, 1).astype(
        jnp.float32
    )
    from_above = from_behind(window[:, :, :piece].astype(jnp.bfloat16), BLK, -1).astype(jnp.float32)
    total = own_part + from_below + from_above
    return (total[0], total[1])


def attend_forward(queries, all_keys, all_values, picker, live_rows):
    shaped = queries.reshape(all_keys.shape[0], SLOTS, -1, HEADS, HD)
    key_sel = pick_slots(picker, all_keys)
    value_sel = pick_slots(picker, all_values)
    scores = jnp.einsum(
        "spqhd,sphkd->sphqk", shaped, key_sel, preferred_element_type=jnp.float32
    ) * HD ** (-0.5)
    row_max = jnp.max(scores, axis=-1, keepdims=True)
    log_total = row_max + jnp.log(jnp.sum(jnp.exp(scores - row_max), axis=-1, keepdims=True))
    weights_low = jnp.exp(scores - log_total).astype(jnp.bfloat16)
    mixed_heads = jnp.einsum(
        "sphqk,sphkd->spqhd", weights_low, value_sel, preferred_element_type=jnp.float32
    )
    mixed_heads = mixed_heads * live_rows[:, :, None, None, None].astype(jnp.float32)
    return (mixed_heads.reshape(queries.shape), log_total)


def attend_backward(queries, all_keys, all_values, log_total, grad_mixed, picker, live_rows):
    scale_factor = HD ** (-0.5)
    shaped = queries.reshape(all_keys.shape[0], SLOTS, -1, HEADS, HD)
    grad_shaped = grad_mixed.reshape(shaped.shape) * live_rows[:, :, None, None, None]
    key_sel = pick_slots(picker, all_keys)
    value_sel = pick_slots(picker, all_values)
    scores = (
        jnp.einsum("spqhd,sphkd->sphqk", shaped, key_sel, preferred_element_type=jnp.float32)
        * scale_factor
    )
    weights_full = jnp.exp(scores - log_total)
    grad_weights = jnp.einsum(
        "spqhd,sphkd->sphqk", grad_shaped, value_sel, preferred_element_type=jnp.float32
    )
    delta_rows = jnp.sum(weights_full * grad_weights, axis=-1, keepdims=True)
    grad_scores = (weights_full * (grad_weights - delta_rows)).astype(jnp.bfloat16)
    grad_query = (
        jnp.einsum("sphqk,sphkd->spqhd", grad_scores, key_sel, preferred_element_type=jnp.float32)
        * scale_factor
    )
    grad_key_sel = (
        jnp.einsum("sphqk,spqhd->sphkd", grad_scores, shaped, preferred_element_type=jnp.float32)
        * scale_factor
    )
    grad_value_sel = jnp.einsum(
        "sphqk,spqhd->sphkd",
        weights_full.astype(jnp.bfloat16),
        grad_shaped,
        preferred_element_type=jnp.float32,
    )
    picker_wide = picker.astype(jnp.float32)
    grad_keys = jnp.einsum(
        "spht,sphkd->stkhd", picker_wide, grad_key_sel, precision=lax.Precision.HIGHEST
    ).reshape(all_keys.shape)
    grad_values = jnp.einsum(
        "spht,sphkd->stkhd", picker_wide, grad_value_sel, precision=lax.Precision.HIGHEST
    ).reshape(all_values.shape)
    return (grad_query.reshape(queries.shape), grad_keys, grad_values)


def layer_forward(hidden_in, weights, picker, live_rows, swapped):
    (
        query_weight,
        key_weight,
        value_weight,
        output_weight,
        query_bias,
        value_bias,
        output_bias,
        expand_weight,
        expand_bias,
        reduce_weight,
        reduce_bias,
        first_gain,
        first_shift,
        second_gain,
        second_shift,
    ) = weights
    seq_count = live_rows.shape[0]
    hidden_low = hidden_in.astype(jnp.bfloat16)
    queries = (matmul(hidden_low, query_weight) + query_bias.astype(jnp.float32)).astype(
        jnp.bfloat16
    )
    key_local = matmul(hidden_low, key_weight).astype(jnp.bfloat16).reshape(seq_count, -1, D)
    value_local = (
        (matmul(hidden_low, value_weight) + value_bias.astype(jnp.float32))
        .astype(jnp.bfloat16)
        .reshape(seq_count, -1, D)
    )
    if swapped:
        all_keys, all_values = side_by_side((key_local, value_local), BLK, 1, 0)
    else:
        all_keys, all_values = neighbour_rows(key_local, value_local)
    mixed_heads, log_total = attend_forward(queries, all_keys, all_values, picker, live_rows)
    mixed_low = mixed_heads.astype(jnp.bfloat16)
    attn_out = matmul(mixed_low, output_weight) + output_bias.astype(jnp.float32)
    first_norm, normed_one, inv_std_one = norm_forward(
        hidden_in + attn_out, first_gain.astype(jnp.float32), first_shift.astype(jnp.float32)
    )
    first_low = first_norm.astype(jnp.bfloat16)
    inner_pre = matmul(first_low, expand_weight) + expand_bias.astype(jnp.float32)
    act_low = jax.nn.gelu(inner_pre, approximate=False).astype(jnp.bfloat16)
    outer_out = matmul(act_low, reduce_weight) + reduce_bias.astype(jnp.float32)
    layer_out, normed_two, inv_std_two = norm_forward(
        first_norm + outer_out, second_gain.astype(jnp.float32), second_shift.astype(jnp.float32)
    )
    saved = (
        hidden_low,
        queries,
        key_local,
        value_local,
        all_keys,
        all_values,
        log_total,
        mixed_low,
        normed_one,
        inv_std_one,
        first_low,
        inner_pre,
        act_low,
        normed_two,
        inv_std_two,
    )
    return (layer_out, saved)


def reduce_grads(grads):
    return jax.tree.map(
        lambda part: summed_rows(part, ("dp_0", "dp_1", "dp_2", "blk_0"), "blk_1", 0), grads
    )


def layer_backward(grad_out, weights, saved, picker, live_rows, swapped):
    (
        query_weight,
        key_weight,
        value_weight,
        output_weight,
        query_bias,
        value_bias,
        output_bias,
        expand_weight,
        expand_bias,
        reduce_weight,
        reduce_bias,
        first_gain,
        first_shift,
        second_gain,
        second_shift,
    ) = weights
    (
        hidden_low,
        queries,
        key_local,
        value_local,
        all_keys,
        all_values,
        log_total,
        mixed_low,
        normed_one,
        inv_std_one,
        first_low,
        inner_pre,
        act_low,
        normed_two,
        inv_std_two,
    ) = saved
    grad_second, grad_second_gain, grad_second_shift = norm_backward(
        grad_out, second_gain.astype(jnp.float32), normed_two, inv_std_two
    )
    grad_outer = grad_second.astype(jnp.bfloat16)
    grad_reduce_weight = contract_rows(act_low, grad_outer)
    grad_reduce_bias = jnp.sum(grad_outer.astype(jnp.float32), axis=0)
    grad_inner = (times_transpose(grad_outer, reduce_weight) * gelu_slope(inner_pre)).astype(
        jnp.bfloat16
    )
    grad_expand_weight = contract_rows(first_low, grad_inner)
    grad_expand_bias = jnp.sum(grad_inner.astype(jnp.float32), axis=0)
    grad_first = grad_second + times_transpose(grad_inner, expand_weight)
    grad_residual, grad_first_gain, grad_first_shift = norm_backward(
        grad_first, first_gain.astype(jnp.float32), normed_one, inv_std_one
    )
    grad_attn = grad_residual.astype(jnp.bfloat16)
    grad_output_weight = contract_rows(mixed_low, grad_attn)
    grad_output_bias = jnp.sum(grad_attn.astype(jnp.float32), axis=0)
    grad_mixed = times_transpose(grad_attn, output_weight).astype(jnp.bfloat16)
    grad_query, grad_keys, grad_values = attend_backward(
        queries, all_keys, all_values, log_total, grad_mixed, picker, live_rows
    )
    if swapped:
        grad_key_local, grad_value_local = tuple(
            (
                part.astype(jnp.float32)
                for part in side_by_side_2(
                    (grad_keys.astype(jnp.bfloat16), grad_values.astype(jnp.bfloat16)), BLK, 1, 0
                )
            )
        )
    else:
        grad_key_local, grad_value_local = return_rims(grad_keys, grad_values, key_local.shape[1])
    query_low = grad_query.astype(jnp.bfloat16)
    key_low = grad_key_local.reshape(-1, D).astype(jnp.bfloat16)
    value_low = grad_value_local.reshape(-1, D).astype(jnp.bfloat16)
    grad_query_weight = contract_rows(hidden_low, query_low)
    grad_key_weight = contract_rows(hidden_low, key_low)
    grad_value_weight = contract_rows(hidden_low, value_low)
    grad_query_bias = jnp.sum(query_low.astype(jnp.float32), axis=0)
    grad_value_bias = jnp.sum(value_low.astype(jnp.float32), axis=0)
    grad_input = (
        grad_residual
        + times_transpose(query_low, query_weight)
        + times_transpose(key_low, key_weight)
        + times_transpose(value_low, value_weight)
    )
    grads = (
        grad_query_weight,
        grad_key_weight,
        grad_value_weight,
        grad_output_weight,
        grad_query_bias,
        grad_value_bias,
        grad_output_bias,
        grad_expand_weight,
        grad_expand_bias,
        grad_reduce_weight,
        grad_reduce_bias,
        grad_first_gain,
        grad_first_shift,
        grad_second_gain,
        grad_second_shift,
    )
    return (grad_input, reduce_grads(grads))


def local(
    hidden,
    output_grad,
    block_counts,
    slot_table,
    block_order_two,
    block_order_three,
    query_weight,
    key_weight,
    value_weight,
    output_weight,
    query_bias,
    value_bias,
    output_bias,
    expand_weight,
    expand_bias,
    reduce_weight,
    reduce_bias,
    first_gain,
    first_shift,
    second_gain,
    second_shift,
):
    seq_count, row_count, model_width = hidden.shape
    piece_rows = row_count // SLOTS
    block_index = lax.axis_index(BLK)
    piece_slot = (SLOTS * block_index + jnp.arange(SLOTS, dtype=jnp.int32)) * piece_rows // BLOCK
    block_number, live_rows = live_pieces(slot_table, block_counts, piece_slot)
    picker_one = selection(
        slot_table, block_counts, block_order_two, block_order_three, block_number, False
    )
    picker_two = selection(
        slot_table, block_counts, block_order_two, block_order_three, block_number, True
    )
    stacked = (
        query_weight,
        key_weight,
        value_weight,
        output_weight,
        query_bias,
        value_bias,
        output_bias,
        expand_weight,
        expand_bias,
        reduce_weight,
        reduce_bias,
        first_gain,
        first_shift,
        second_gain,
        second_shift,
    )
    layer_one = tuple((tensor[0] for tensor in stacked))
    layer_two = tuple((tensor[1] for tensor in stacked))
    hidden_flat = hidden.reshape(-1, model_width).astype(jnp.float32)
    middle, saved_one = layer_forward(hidden_flat, layer_one, picker_one, live_rows, False)
    final_out, saved_two = layer_forward(middle, layer_two, picker_two, live_rows, True)
    grad_middle, reduced_two = layer_backward(
        output_grad.reshape(-1, model_width).astype(jnp.float32),
        layer_two,
        saved_two,
        picker_two,
        live_rows,
        True,
    )
    grad_hidden, reduced_one = layer_backward(
        grad_middle, layer_one, saved_one, picker_one, live_rows, False
    )
    stacked_grads = tuple(
        (
            jnp.stack([first_part, second_part])
            for first_part, second_part in zip(reduced_one, reduced_two)
        )
    )
    return (
        final_out.astype(jnp.bfloat16).reshape(hidden.shape),
        grad_hidden.astype(jnp.bfloat16).reshape(hidden.shape),
    ) + stacked_grads


def solution(mesh):
    finer = Mesh(mesh.devices.reshape(4, 4, 2, 2, 2), ("dp_0", "dp_1", "dp_2", "blk_0", "blk_1"))
    in_specs = (
        P(DP, BLK, None),
        P(DP, BLK, None),
        P(DP),
        P(DP, None),
        P(),
        P(),
        P(),
        P(),
        P(),
        P(),
        P(),
        P(),
        P(),
        P(),
        P(),
        P(),
        P(),
        P(),
        P(),
        P(),
        P(),
    )
    out_specs = (
        P(DP, BLK, None),
        P(DP, BLK, None),
        P(None, DP_BLK, None),
        P(None, DP_BLK, None),
        P(None, DP_BLK, None),
        P(None, DP_BLK, None),
        P(None, DP_BLK),
        P(None, DP_BLK),
        P(None, DP_BLK),
        P(None, DP_BLK, None),
        P(None, DP_BLK),
        P(None, DP_BLK, None),
        P(None, DP_BLK),
        P(None, DP_BLK),
        P(None, DP_BLK),
        P(None, DP_BLK),
        P(None, DP_BLK),
    )
    return jax.shard_map(local, mesh=finer, in_specs=in_specs, out_specs=out_specs, check_vma=False)
```

profile of v0, /device:TPU:1, one launch (start us, length us, event | category | flops | bytes accessed | tf_op | source)
XLA Modules:
  0.0 1843.4 jit_solution(50794237182937943)
XLA Ops:
  82.0 13.5 fusion.18
  108.2 35.3 %all-gather.2.cloned.1.call-done = bf16[2,1536,768]{2,1,0:T(8,128)(2,1)} async-done(((bf16[2,384,768]{2,1,0:T(8,128)(2,1)}), bf16[2,1536,768]{2,1,0:T(8,128)(2,1)}) %all-gather.2.cloned.1.call-update) | async-done | bytes 4718608 | tf_op jit(solution)/shard_map/all_gather | solution.py:44
  192.7 11.9 fusion.21
  241.8 9.6 convert_bitcast_fusion.1
  263.0 13.0 convert_bitcast_fusion
  312.6 34.0 %reduce-scatter.98.cloned.1.call-done = bf16[2,384,768]{2,1,0:T(8,128)(2,1)} async-done(((bf16[2,1536,768]{2,1,0:T(8,128)(2,1)}), bf16[2,384,768]{2,1,0:T(8,128)(2,1)}) %reduce-scatter.98.cloned.1.call-update) | async-done | bytes 1179664 | tf_op jit(solution)/shard_map/reduce_scatter | solution.py:70
  480.9 10.2 collective-permute-done.2
  528.6 10.4 reshape_reshape.90
  539.0 13.6 copy.454
  553.3 9.7 fusion.302
  563.0 11.0 reshape_reshape.89
  574.0 13.5 copy.453
  608.9 10.2 reduce-scatter.162.cloned.1.call-done
  619.9 13.5 reduce-scatter.130.cloned.1.call-done
  634.2 12.9 reduce-scatter.138.cloned.1.call-done
  648.0 12.9 reduce-scatter.150.cloned.1.call-done
  661.8 13.1 reduce-scatter.154.cloned.1.call-done
  675.7 12.9 reduce-scatter.146.cloned.1.call-done
  689.5 13.1 reduce-scatter.158.cloned.1.call-done
  703.4 13.1 reduce-scatter.142.cloned.1.call-done
  720.3 10.7 reduce-scatter.128.cloned.1.call-done
  731.8 13.0 reduce-scatter.136.cloned.1.call-done
  745.6 13.1 reduce-scatter.148.cloned.1.call-done
  759.6 13.0 reduce-scatter.152.cloned.1.call-done
  773.3 12.9 reduce-scatter.144.cloned.1.call-done
  787.1 13.1 reduce-scatter.156.cloned.1.call-done
  801.0 13.1 reduce-scatter.160.cloned.1.call-done
  814.9 13.5 reduce-scatter.134.cloned.1.call-done
  829.3 13.1 reduce-scatter.140.cloned.1.call-done
  857.1 299.8 %all-reduce.29 = (f32[64,6]{0,1:T(8,128)S(1)}, f32[64,6]{0,1:T(8,128)S(1)}, f32[64,6]{0,1:T(8,128)S(1)}, f32[64,6]{0,1:T(8,128)S(1)}, f32[64,6]{0,1:T(8,128)S(1)...) all-reduce(f32[64,6]{0,1:T(8,128)S(1)} %copy.526, ...), channel_id=22, replica_groups=mesh['dp_0'=4,'dp_1'=4,'dp_2'=2,'blk_0'=2,'blk_1'=2] {'dp_0','dp_1','dp_..., use_global_device_ids=true, to_apply=%region_50.51.clone | all-reduce | flops 9216 | bytes 73728
  1176.7 351.2 %reduce-scatter.122.cloned.1.call-done = f32[1,24,768]{2,1,0:T(8,128)} async-done(((f32[64,24,768]{2,1,0:T(8,128)}), f32[1,24,768]{2,1,0:T(8,128)}) %reduce-scatter.122.cloned.1.call-update) | async-done | bytes 73744 | tf_op jit(solution)/shard_map/reduce_scatter | solution.py:60
  1529.5 287.6 %all-reduce.33.cloned.1.call-done = (f32[64,6,768]{2,0,1:T(8,128)}, f32[64,6,768]{2,0,1:T(8,128)}, f32[64,6,768]{2,0,1:T(8,128)}, f32[64,6,768]{2,0,1:T(8,128)},...) async-done(((f32[64,6,768]{2,0,1:T(8,128)}, ...) | async-done | bytes 18874384
  (613 shorter events, 484.1 us)
Async XLA Ops:
  7.2 136.3 %all-gather.2.cloned.1.call-start = ((), (), s32[]{:S(2)}) async-start(), calls=%async_computation.33 | async-start | bytes 5898240 | tf_op jit(solution)/shard_map/all_gather | solution.py:44
  102.0 244.6 %reduce-scatter.98.cloned.1.call-start = ((), (), s32[]{:S(2)}) async-start(), calls=%async_computation.34 | async-start | bytes 5898240 | tf_op jit(solution)/shard_map/reduce_scatter | solution.py:70
  292.8 313.3 %reduce-scatter.124.cloned.1.call-start = ((), (), s32[]{:S(2)}) async-start(), calls=%async_computation.47 | async-start | bytes 14155776 | tf_op jit(solution)/shard_map/reduce_scatter | solution.py:59
  302.7 303.9 %reduce-scatter.120.cloned.1.call-start = ((), (), s32[]{:S(2)}) async-start(), calls=%async_computation.45 | async-start | bytes 14155776 | tf_op jit(solution)/shard_map/reduce_scatter | solution.py:59
  360.9 246.5 %reduce-scatter.102.cloned.1.call-start = ((), (), s32[]{:S(2)}) async-start(), calls=%async_computation.36 | async-start | bytes 3538944 | tf_op jit(solution)/shard_map/reduce_scatter | solution.py:59
  365.7 241.7 %reduce-scatter.114.cloned.1.call-start = ((), (), s32[]{:S(2)}) async-start(), calls=%async_computation.42 | async-start | bytes 3538944 | tf_op jit(solution)/shard_map/reduce_scatter | solution.py:59
  369.7 237.7 %reduce-scatter.110.cloned.1.call-start = ((), (), s32[]{:S(2)}) async-start(), calls=%async_computation.40 | async-start | bytes 3538944 | tf_op jit(solution)/shard_map/reduce_scatter | solution.py:59
  373.4 234.1 %reduce-scatter.106.cloned.1.call-start = ((), (), s32[]{:S(2)}) async-start(), calls=%async_computation.38 | async-start | bytes 3538944 | tf_op jit(solution)/shard_map/reduce_scatter | solution.py:59
  375.8 231.7 %reduce-scatter.112.cloned.1.call-start = ((), (), s32[]{:S(2)}) async-start(), calls=%async_computation.41 | async-start | bytes 3538944 | tf_op jit(solution)/shard_map/reduce_scatter | solution.py:59
  395.0 212.5 %reduce-scatter.100.cloned.1.call-start = ((), (), s32[]{:S(2)}) async-start(), calls=%async_computation.35 | async-start | bytes 3538944 | tf_op jit(solution)/shard_map/reduce_scatter | solution.py:59
  426.7 180.8 %reduce-scatter.104.cloned.1.call-start = ((), (), s32[]{:S(2)}) async-start(), calls=%async_computation.37 | async-start | bytes 3538944 | tf_op jit(solution)/shard_map/reduce_scatter | solution.py:59
  508.2 99.3 %reduce-scatter.108.cloned.1.call-start = ((), (), s32[]{:S(2)}) async-start(), calls=%async_computation.39 | async-start | bytes 3538944 | tf_op jit(solution)/shard_map/reduce_scatter | solution.py:59
  519.5 88.0 %reduce-scatter.118.cloned.1.call-start = ((), (), s32[]{:S(2)}) async-start(), calls=%async_computation.44 | async-start | bytes 14155776 | tf_op jit(solution)/shard_map/reduce_scatter | solution.py:59
  590.4 56.8 %reduce-scatter.138.cloned.1.call-start = ((), (), s32[]{:S(2)}) async-start(), calls=%async_computation.54 | async-start | bytes 98304
  591.3 69.7 %reduce-scatter.150.cloned.1.call-start = ((), (), s32[]{:S(2)}) async-start(), calls=%async_computation.60 | async-start | bytes 98304
  592.2 82.7 %reduce-scatter.154.cloned.1.call-start = ((), (), s32[]{:S(2)}) async-start(), calls=%async_computation.62 | async-start | bytes 98304
  593.0 95.6 %reduce-scatter.146.cloned.1.call-start = ((), (), s32[]{:S(2)}) async-start(), calls=%async_computation.58 | async-start | bytes 98304
  593.9 108.7 %reduce-scatter.158.cloned.1.call-start = ((), (), s32[]{:S(2)}) async-start(), calls=%async_computation.64 | async-start | bytes 98304
  594.8 121.7 %reduce-scatter.142.cloned.1.call-start = ((), (), s32[]{:S(2)}) async-start(), calls=%async_computation.56 | async-start | bytes 98304
  595.6 135.4 %reduce-scatter.128.cloned.1.call-start = ((), (), s32[]{:S(2)}) async-start(), calls=%async_computation.49 | async-start | bytes 98304
  596.5 148.3 %reduce-scatter.136.cloned.1.call-start = ((), (), s32[]{:S(2)}) async-start(), calls=%async_computation.53 | async-start | bytes 98304
  597.4 161.4 %reduce-scatter.148.cloned.1.call-start = ((), (), s32[]{:S(2)}) async-start(), calls=%async_computation.59 | async-start | bytes 98304
  598.2 174.3 %reduce-scatter.152.cloned.1.call-start = ((), (), s32[]{:S(2)}) async-start(), calls=%async_computation.61 | async-start | bytes 98304
  599.1 187.2 %reduce-scatter.144.cloned.1.call-start = ((), (), s32[]{:S(2)}) async-start(), calls=%async_computation.57 | async-start | bytes 98304
  599.9 200.2 %reduce-scatter.156.cloned.1.call-start = ((), (), s32[]{:S(2)}) async-start(), calls=%async_computation.63 | async-start | bytes 98304
  600.8 213.3 %reduce-scatter.160.cloned.1.call-start = ((), (), s32[]{:S(2)}) async-start(), calls=%async_computation.65 | async-start | bytes 98304
  601.7 226.8 %reduce-scatter.134.cloned.1.call-start = ((), (), s32[]{:S(2)}) async-start(), calls=%async_computation.52 | async-start | bytes 98304
  603.8 238.6 %reduce-scatter.140.cloned.1.call-start = ((), (), s32[]{:S(2)}) async-start(), calls=%async_computation.55 | async-start | bytes 98304
  604.7 251.6 %reduce-scatter.132.cloned.1.call-start = ((), (), s32[]{:S(2)}) async-start(), calls=%async_computation.51 | async-start | bytes 98304
  606.0 570.7 %reduce-scatter.126.cloned.1.call-start = ((), (), s32[]{:S(2)}) async-start(), calls=%async_computation.48 | async-start | bytes 4792320 | tf_op jit(solution)/shard_map/reduce_scatter | solution.py:60
  606.6 921.3 %reduce-scatter.122.cloned.1.call-start = ((), (), s32[]{:S(2)}) async-start(), calls=%async_computation.46 | async-start | bytes 4792320 | tf_op jit(solution)/shard_map/reduce_scatter | solution.py:60
  607.3 1209.8 %all-reduce.33.cloned.1.call-start = ((), (), s32[]{:S(2)}) async-start(), calls=%async_computation.67 | async-start | bytes 37748736
  (126 other events, 1337.3 us)
Sparse Core Ops, SparseCore 0:
  102.2 41.2 all-gather.1
  292.9 53.7 reduce-scatter.97
  349.2 20.2 reduce-scatter.123
  371.9 21.9 reduce-scatter.119
  396.2 14.0 reduce-scatter.101
  412.4 13.9 reduce-scatter.113
  428.9 13.9 reduce-scatter.109
  445.2 13.9 reduce-scatter.105
  461.6 13.9 reduce-scatter.111
  477.8 13.9 reduce-scatter.99
  521.3 13.9 reduce-scatter.107
  552.8 17.8 reduce-scatter.117
  587.7 17.2 reduce-scatter.115
  607.3 11.6 reduce-scatter.161
  621.9 11.4 reduce-scatter.129
  635.6 11.4 reduce-scatter.137
  649.4 11.4 reduce-scatter.149
  663.3 11.4 reduce-scatter.153
  677.1 11.4 reduce-scatter.145
  691.0 11.4 reduce-scatter.157
  705.0 11.4 reduce-scatter.141
  719.5 11.4 reduce-scatter.127
  733.3 11.4 reduce-scatter.135
  747.2 11.4 reduce-scatter.147
  761.0 11.4 reduce-scatter.151
  788.7 11.4 reduce-scatter.155
  802.6 11.4 reduce-scatter.159
  816.9 11.4 reduce-scatter.133
  830.9 11.4 reduce-scatter.139
  858.7 311.0 reduce-scatter.125
  1172.3 355.5 reduce-scatter.121
  1535.5 281.5 all-reduce.32
  (3 shorter events, 33.5 us)
where the time goes:
time: 1860 us; the launch traced here: 1840 us
  waiting for transfers between devices  958 us (52%)
  blocking collectives  300 us (16%)
  local copies, waits for them, and re-layouts  278 us (15%)
  matrix products  225 us (12%)
  other arithmetic  49.4 us (3%)
    unnamed x54, waiting for transfers between devices  515 us
    reduce_scatter x2, waiting for transfers between devices, summed_rows(): return lax.psum_scatter(pieces, chips, scatter_dimension=0, tiled=True)[0]  351 us
    unnamed x1, blocking collectives  300 us
    unnamed x305, local copies, waits for them, and re-layouts  74.2 us
    transpose x12, local copies, waits for them, and re-layouts, summed_rows(): pieces = pieces.reshape(*sizes, *inside).swapaxes(0, 1).reshape(-1, *inside)  61.2 us
    dot_general x12, matrix products, matmul(): return jnp.dot(left, right, preferred_element_type=jnp.float32)  39.1 us
    dot_general x12, matrix products, contract_rows(): lax.dot_general(left, right, (((0,), (0,)), ((), ())), preferred_element_...  37.4 us
  transfers between devices with their start and end apart: 39, of which 26 were waited for; matrix products, arithmetic and copies ran while one was open for 16% of the time, Pallas kernels for 0%

commit v1 on v0

--- a/solution.py
+++ b/solution.py
@@ -1,6 +1,8 @@
 import jax
 import jax.numpy as jnp
 from jax import lax
+from jax.experimental import pallas as pl
+from jax.experimental.pallas import tpu as pltpu
 from jax.sharding import Mesh
 from jax.sharding import PartitionSpec as P
 
@@ -15,6 +17,9 @@
 
 
 EPSILON = 1e-06
+MESH = pl.DeviceIdType.MESH
+BF = jnp.bfloat16
+F32 = jnp.float32
 ROOT_HALF = 0.7071067811865476
 INV_ROOT_TAU = 0.3989422804014327
 
@@ -311,9 +316,233 @@
     return (layer_out, saved)
 
 
+def peer_of(axis, place, offset):
+    at = lax.rem(place[axis] + offset, 4)
+    if axis == 0:
+        return {"dp_0": at}
+    if axis == 1:
+        return {"dp_1": at}
+    return {"dp_2": lax.rem(at, 2), "blk_0": at // 2}
+
+
+ORDERS = ((0, 1, 2), (1, 2, 0), (2, 0, 1))
+
+
+def piece(ref, part, at, core):
+    z, x, y = at
+    if part < 2:
+        return ref.at[pl.ds(pl.multiple_of((z * 4 + x) * 48, 16), 48), pl.ds(pl.multiple_of(y * 768 + core * 384, 128), 384)]
+    yy = lax.rem(y, 2) * 2 + y // 2
+    return ref.at[pl.ds(pl.multiple_of((z * 4 + x) * 192 + yy * 48, 16), 48), pl.ds(pl.multiple_of(core * 384, 128), 384)]
+
+
+def block(ref, part, a1, core):
+    order = ORDERS[part]
+    out = []
+    for b in range(4):
+        for c in range(4):
+            at = [None, None, None]
+            at[order[0]], at[order[1]], at[order[2]] = a1, b, c
+            out.append((piece(ref, part, at, core), (b, c)))
+    return out
+
+
+def scatter_kernel(
+    p0, p1, p2, vec,
+    q_out, r_out, v_out,
+    mine, theirs, got1, sum1, got2, sum2, got3, last, fix_send, fix_got, rfix_send, rfix_got,
+    vcore, vy, vz, vx, vsum,
+    local_sem, send0, recv0, send1, recv1, send2, recv2, send3, recv3, fsend, frecv, vsend, vrecv,
+):
+    z, x = lax.axis_index("dp_0"), lax.axis_index("dp_1")
+    y_lo, y_hi, core = lax.axis_index("dp_2"), lax.axis_index("blk_0"), lax.axis_index("blk_1")
+    place = (z, x, y_hi * 2 + y_lo)
+    pos = y_lo * 4 + y_hi * 2 + core
+    other = 1 - core
+    grads = (p0, p1, p2)
+
+    barrier = pltpu.get_barrier_semaphore()
+    peers = [peer_of(a, place, d) for a in (0, 1) for d in (1, 2, 3)]
+    for d in range(1, 8):
+        t = lax.rem(pos + d, 8)
+        peers.append({"dp_2": t // 4, "blk_0": lax.rem(t // 2, 2), "blk_1": lax.rem(t, 2)})
+    for p in peers:
+        pl.semaphore_signal(barrier, inc=1, device_id=p, device_id_type=MESH)
+    pl.semaphore_wait(barrier, len(peers))
+
+    def remote(src, dst, s, r, device):
+        return pltpu.make_async_remote_copy(src_ref=src, dst_ref=dst, send_sem=s, recv_sem=r, device_id=device, device_id_type=MESH)
+
+    sibling = {"blk_1": other}
+    vc = remote(vec, vcore, vsend.at[0], vrecv.at[0], sibling)
+    vc.start()
+    halves = {}
+    for i in (1, 2, 3, 0):
+        for part in range(3):
+            a1 = lax.rem(place[ORDERS[part][0]] + i, 4)
+            for k, (src, (b, c)) in enumerate(block(grads[part], part, a1, other)):
+                halves[part, i, k] = remote(src, theirs.at[part, i, b, c], send0.at[part, i], recv0.at[part, i], sibling)
+                halves[part, i, k].start()
+            for k, (src, (b, c)) in enumerate(block(grads[part], part, a1, core)):
+                pltpu.make_async_copy(src, mine.at[part, i, b, c], local_sem.at[part, i]).start()
+
+    def wait_all(part, i):
+        whole = theirs.at[part, i]
+        pltpu.make_async_copy(whole, mine.at[part, i], local_sem.at[part, i]).wait()
+        remote(whole, whole, send0.at[part, i], recv0.at[part, i], sibling).wait()
+
+    first = {}
+    for i in (1, 2, 3, 0):
+        for part in range(3):
+            wait_all(part, i)
+
+            @pl.loop(0, 16)
+            def _(k, part=part, i=i):
+                b, c = k // 4, lax.rem(k, 4)
+                mine[part, i, b, c] = mine[part, i, b, c] + theirs[part, i, b, c]
+
+            if i:
+                first[part, i] = remote(mine.at[part, i], got1.at[part, i - 1], send1.at[part, i - 1], recv1.at[part, i - 1], peer_of(ORDERS[part][0], place, i))
+                first[part, i].start()
+    vc.wait()
+    vsum[...] = vec[...] + vcore[...]
+    vys = [remote(vsum, vy.at[d - 1], vsend.at[d], vrecv.at[d], peer_of(2, place, d)) for d in (1, 2, 3)]
+    for c in vys:
+        c.start()
+    second = {}
+    for part in range(3):
+        for i in (1, 2, 3):
+            first[part, i].wait()
+        a = ORDERS[part][1]
+
+        @pl.loop(0, 16)
+        def _(k, part=part):
+            b, c = k // 4, lax.rem(k, 4)
+            total = mine[part, 0, b, c].astype(F32) + got1[part, 0, b, c].astype(F32)
+            total += got1[part, 1, b, c].astype(F32) + got1[part, 2, b, c].astype(F32)
+            sum1[part, b, c] = total.astype(BF)
+
+        for i in (1, 2, 3):
+            at = lax.rem(place[a] + i, 4)
+            second[part, i] = remote(sum1.at[part, at], got2.at[part, i - 1], send2.at[part, i - 1], recv2.at[part, i - 1], peer_of(a, place, i))
+            second[part, i].start()
+    for c in vys:
+        c.wait()
+    vsum[...] = vsum[...] + vy[0] + vy[1] + vy[2]
+    vzs = []
+    for d in (1, 2, 3):
+        at = lax.rem(z + d, 4)
+        vzs.append(remote(vsum.at[pl.ds(pl.multiple_of(at * 32, 8), 32)], vz.at[d - 1], vsend.at[3 + d], vrecv.at[3 + d], peer_of(0, place, d)))
+        vzs[-1].start()
+    third = {}
+    for part in range(3):
+        for i in (1, 2, 3):
+            second[part, i].wait()
+        a = ORDERS[part][1]
+        own = place[a]
+        for c in range(4):
+            total = sum1[part, own, c].astype(F32) + got2[part, 0, c].astype(F32)
+            total += got2[part, 1, c].astype(F32) + got2[part, 2, c].astype(F32)
+            sum2[part, c] = total.astype(BF)
+        a = ORDERS[part][2]
+        for i in (1, 2, 3):
+            at = lax.rem(place[a] + i, 4)
+            third[part, i] = remote(sum2.at[part, at], got3.at[part, i - 1], send3.at[part, i - 1], recv3.at[part, i - 1], peer_of(a, place, i))
+            third[part, i].start()
+    for c in vzs:
+        c.wait()
+    vrow = vsum[pl.ds(pl.multiple_of(z * 32, 8), 32)] + vz[0] + vz[1] + vz[2]
+    vsum[0:32] = vrow
+    vxs = []
+    for d in (1, 2, 3):
+        at = lax.rem(x + d, 4)
+        vxs.append(remote(vsum.at[pl.ds(pl.multiple_of(at * 8, 8), 8)], vx.at[d - 1], vsend.at[6 + d], vrecv.at[6 + d], peer_of(1, place, d)))
+        vxs[-1].start()
+    for part in range(3):
+        for i in (1, 2, 3):
+            third[part, i].wait()
+        own = place[ORDERS[part][2]]
+        total = sum2[part, own].astype(F32) + got3[part, 0].astype(F32) + got3[part, 1].astype(F32) + got3[part, 2].astype(F32)
+        if part < 2:
+            for k in range(8):
+                fix_send[k, part, 0:6] = total[6 * k : 6 * k + 6]
+        else:
+            rfix_send[...] = total
+    fixes = []
+    for d in range(1, 8):
+        t = lax.rem(pos + d, 8)
+        device = {"dp_2": t // 4, "blk_0": lax.rem(t // 2, 2), "blk_1": lax.rem(t, 2)}
+        fixes.append(remote(fix_send.at[t], fix_got.at[pos], fsend.at[d], frecv.at[d], device))
+        fixes[-1].start()
+    there = pl.multiple_of(other * 24, 8)
+    here = pl.multiple_of(core * 24, 8)
+    rfix = remote(rfix_send.at[pl.ds(there, 24)], rfix_got, fsend.at[0], frecv.at[0], sibling)
+    rfix.start()
+    for c in vxs:
+        c.wait()
+    v_out[...] = vsum[pl.ds(pl.multiple_of(x * 8, 8), 8)] + vx[0] + vx[1] + vx[2]
+    rfix.wait()
+    for c in fixes:
+        c.wait()
+    fix_got[pos] = fix_send[pos]
+    for s in range(8):
+        y, c = (s // 2 % 2) * 2 + s // 4, s % 2
+        for part in range(2):
+            q_out[part, y, :, c * 384 : (c + 1) * 384] = fix_got[s, part, 0:6]
+    r_out[:, pl.ds(pl.multiple_of(core * 384, 128), 384)] = rfix_send[pl.ds(here, 24)]
+    r_out[:, pl.ds(pl.multiple_of(other * 384, 128), 384)] = rfix_got[...]
+
+
+def reduce_scatter(p0, p1, p2, vec):
+    dma = pltpu.SemaphoreType.DMA
+    return pl.pallas_call(
+        scatter_kernel,
+        out_shape=(
+            jax.ShapeDtypeStruct((2, 4, 6, 768), F32),
+            jax.ShapeDtypeStruct((24, 768), F32),
+            jax.ShapeDtypeStruct((8, 128), F32),
+        ),
+        in_specs=[pl.BlockSpec(memory_space=pl.ANY)] * 3 + [pl.BlockSpec(memory_space=pltpu.VMEM)],
+        out_specs=[pl.BlockSpec(memory_space=pltpu.VMEM)] * 3,
+        scratch_shapes=[
+            pltpu.VMEM((3, 4, 4, 4, 48, 384), BF),
+            pltpu.VMEM((3, 4, 4, 4, 48, 384), BF),
+            pltpu.VMEM((3, 3, 4, 4, 48, 384), BF),
+            pltpu.VMEM((3, 4, 4, 48, 384), BF),
+            pltpu.VMEM((3, 3, 4, 48, 384), BF),
+            pltpu.VMEM((3, 4, 48, 384), BF),
+            pltpu.VMEM((3, 3, 48, 384), BF),
+            pltpu.VMEM((8, 128), F32),
+            pltpu.VMEM((8, 2, 8, 384), F32),
+            pltpu.VMEM((8, 2, 8, 384), F32),
+            pltpu.VMEM((48, 384), F32),
+            pltpu.VMEM((24, 384), F32),
+            pltpu.VMEM((128, 128), F32),
+            pltpu.VMEM((3, 128, 128), F32),
+            pltpu.VMEM((3, 32, 128), F32),
+            pltpu.VMEM((3, 8, 128), F32),
+            pltpu.VMEM((128, 128), F32),
+            dma((3, 4)), dma((3, 4)), dma((3, 4)),
+            dma((3, 3)), dma((3, 3)), dma((3, 3)), dma((3, 3)), dma((3, 3)), dma((3, 3)),
+            dma((8,)), dma((8,)), dma((10,)), dma((10,)),
+        ],
+        compiler_params=pltpu.CompilerParams(collective_id=0, has_side_effects=True, vmem_limit_bytes=56 * 1024 * 1024),
+    )(p0, p1, p2, vec)
+
+
 def reduce_grads(grads):
-    return jax.tree.map(
-        lambda part: summed_rows(part, ("dp_0", "dp_1", "dp_2", "blk_0"), "blk_1", 0), grads
+    (gq, gk, gv, go, gqb, gvb, gob, ge, geb, gr, grb, gfg, gfs, gsg, gss) = grads
+    p0 = jnp.concatenate([gq.astype(BF), gk.astype(BF), gv.astype(BF), go.astype(BF)], axis=1)
+    vecs = [v.reshape(128, -1) for v in (gqb, gvb, gob, grb, gfg, gfs, gsg, gss, geb)]
+    vec = jnp.concatenate(vecs + [jnp.zeros((128, 128 - 72), F32)], axis=1)
+    quads, r_rows, v_rows = reduce_scatter(p0, ge.astype(BF), gr.astype(BF), vec)
+    pos = lax.axis_index("dp_2") * 4 + lax.axis_index("blk_0") * 2 + lax.axis_index("blk_1")
+    row = lax.dynamic_index_in_dim(v_rows, pos, 0, keepdims=False)
+    small = [row[6 * i : 6 * i + 6] for i in range(8)]
+    e_rows = quads[1].transpose(1, 0, 2).reshape(6, 3072)
+    return (
+        quads[0, 0], quads[0, 1], quads[0, 2], quads[0, 3], small[0], small[1], small[2],
+        e_rows, row[48:72], r_rows, small[3], small[4], small[5], small[6], small[7],
     )
 
 

time: 1860 us -> 657 us (0.35)
  waiting for transfers between devices: 958 us -> 67.6 us
  blocking collectives: 300 us -> 0 us
  local copies, waits for them, and re-layouts: 278 us -> 152 us
  Pallas kernels: 0 us -> 119 us
    unnamed x54 -> x3, waiting for transfers between devices: 515 us -> 24.4 us
    reduce_scatter x15 -> x0, waiting for transfers between devices: 385 us -> none  [the longest x2 351 us: summed_rows(): return lax.psum_scatter(pieces, chips, scatter_dimension=0, tiled=True)[0]]
    unnamed x1 -> x0, blocking collectives: 300 us -> none
    pallas_call x0 -> x2, Pallas kernels: none -> 119 us  [reduce_scatter(): pl.pallas_call(scatter_kernel, out_shape=(jax.ShapeDtypeStruct((2, 4, 6,...]
    transpose x12 -> x0, local copies, waits for them, and re-layouts: 61.2 us -> none  [summed_rows(): pieces = pieces.reshape(*sizes, *inside).swapaxes(0, 1).reshape(-1, *inside)]
    another operation x31 -> x11, local copies, waits for them, and re-layouts: 65.9 us -> 30.6 us  [the longest x23 35 us: summed_rows(): pieces = pieces.reshape(*sizes, *inside).swapaxes(0, 1).reshape(-1, *inside)]
    unnamed x305 -> x300, local copies, waits for them, and re-layouts: 74.2 us -> 40.1 us
  transfers between devices with their start and end apart: 39 -> 6, of which waited for: 26 -> 4; matrix products, arithmetic and copies ran while one was open for 16% -> 11% of each run, Pallas kernels for 0% -> 10%
where the time goes in v1:
time: 657 us; the launch traced here: 646 us
  matrix products  217 us (33%)
  local copies, waits for them, and re-layouts  152 us (23%)
  Pallas kernels  119 us (18%)
  waiting for transfers between devices  67.6 us (10%)
  other arithmetic  58.7 us (9%)
  between operations  17.5 us (3%)
  starting transfers between devices  13.5 us (2%)
    pallas_call x2, Pallas kernels, reduce_scatter(): pl.pallas_call(scatter_kernel, out_shape=(jax.ShapeDtypeStruct((2, 4, 6,...  119 us
    dot_general x12, matrix products, matmul(): return jnp.dot(left, right, preferred_element_type=jnp.float32)  41 us
    unnamed x300, local copies, waits for them, and re-layouts  40.1 us
    all_gather x1, waiting for transfers between devices, side_by_side(): filled = lax.all_gather(both, axis, axis=dim, tiled=True)  37 us
    dot_general x12, matrix products, contract_rows(): lax.dot_general(left, right, (((0,), (0,)), ((), ())), preferred_element_...  36.9 us
    dot_general x12, matrix products, times_transpose(): lax.dot_general(left, right, (((1,), (1,)), ((), ())), preferred_element_...  29 us
    another operation x9, local copies, waits for them, and re-layouts  29 us
    dot_general x2, matrix products, attend_backward(): jnp.einsum('spht,sphkd->stkhd', picker_wide, grad_value_sel, precision=la...  26.6 us
  transfers between devices with their start and end apart: 6, of which 4 were waited for; matrix products, arithmetic and copies ran while one was open for 11% of the time, Pallas kernels for 10%

profile of v1, /device:TPU:1, one launch (start us, length us, event | category | flops | bytes accessed | tf_op | source)
XLA Modules:
  0.0 646.0 jit_solution(9478528919751407179)
XLA Ops:
  14.0 6.2 collective-permute-start
  33.7 5.9 collective-permute-done.1
  50.1 6.5 %reshape.813 = bf16[3,512,12,64]{1,0,3,2:T(4,128)(2,1)} reshape(bf16[1,1,1536,768]{2,3,1,0:T(8,128)(2,1)} %get-tuple-element.159) | data formatting | bytes 4718592 | tf_op jit(solution)/shard_map/reshape.12
  74.2 7.5 %fusion.175 = bf16[1,3,128,12,64]{2,4,3,1,0:T(8,128)(2,1)S(1)} fusion(bf16[3,12,512,64]{2,0,3,1:T(4,128)(2,1)S(1)} %convert_bitcast_fusion.5, f32[3,12,128,512]{3,2,1,0:T(8,128)} %copy-done, f32[3,12,128]{2,1,0:T(8,128)S(1)} %log_add_fusion.1, f32[3]{0:T(128)S(1)} %copy-done.97), kind=kOutput, calls=%fused_computation.203 | convolution fusion | flops 309657600 | bytes 12404748 | tf_op jit(solution)/shard_map/sphqk,sphkd->spqhd/dot_general | solution.py:206
  83.5 13.8 %fusion.18 = (bf16[384,3072]{1,0:T(8,128)(2,1)S(1)}, f32[384,3072]{1,0:T(8,128)}) fusion(f32[3072]{0:T(1024)S(1)} %bitcast.409, bf16[2,768,3072]{2,1,0:T(8,128)(2,1)S(1)} %bitcast.420, f32[384,768]{1,0:T(8,128)S(1)} %get-tuple-element.198, f32[768]{0:T(1024)S(1)} %copy-done.98, f32[768]{0:T(1024)S(1)} %copy-done.69, f32[384]{0:T(512)S(1)} %add_rsqrt_fusion.3, ...), kind=kOutput, calls=%fused_computation.39 | convolution fusion | flops 1891270656 | bytes 13000704 | tf_op jit(solution)/shard_map/dot_general | solution.py:80
  107.7 37.0 %all-gather.2.cloned.1.call-done = bf16[2,1536,768]{2,1,0:T(8,128)(2,1)} async-done(((bf16[2,384,768]{2,1,0:T(8,128)(2,1)}), bf16[2,1536,768]{2,1,0:T(8,128)(2,1)}) %all-gather.2.cloned.1.call-update) | async-done | bytes 4718608 | tf_op jit(solution)/shard_map/all_gather | solution.py:49
  153.9 6.5 %reshape.820 = bf16[3,512,12,64]{1,0,3,2:T(4,128)(2,1)} reshape(bf16[1,1536,768]{1,2,0:T(8,128)(2,1)} %copy.226) | data formatting | bytes 4718592 | tf_op jit(solution)/shard_map/reshape.40
  173.9 6.7 %reshape.817 = bf16[3,512,12,64]{1,0,3,2:T(4,128)(2,1)} reshape(bf16[1,1536,768]{1,2,0:T(8,128)(2,1)} %copy.222) | data formatting | bytes 4718592 | tf_op jit(solution)/shard_map/reshape.37
  184.4 7.5 %fusion.172 = bf16[1,3,128,12,64]{2,4,3,1,0:T(8,128)(2,1)S(1)} fusion(bf16[3,12,512,64]{2,0,3,1:T(4,128)(2,1)S(1)} %convert_bitcast_fusion.3, f32[3,12,128,512]{3,2,1,0:T(8,128)} %copy-done.1, f32[3,12,128]{2,1,0:T(8,128)S(1)} %log_add_fusion, f32[3]{0:T(128)S(1)} %copy-done.97), kind=kOutput, calls=%fused_computation.202 | convolution fusion | flops 309657600 | bytes 12404748 | tf_op jit(solution)/shard_map/sphqk,sphkd->spqhd/dot_general | solution.py:206
  193.8 12.0 %fusion.21 = (bf16[384,3072]{1,0:T(8,128)(2,1)S(1)}, f32[384,3072]{1,0:T(8,128)S(1)}) fusion(f32[3072]{0:T(1024)S(1)} %bitcast.411, bf16[2,768,3072]{2,1,0:T(8,128)(2,1)S(1)} %bitcast.422, f32[384,768]{1,0:T(8,128)S(1)} %get-tuple-element.206, f32[768]{0:T(1024)S(1)} %copy-done.100, f32[768]{0:T(1024)S(1)} %copy-done.71, f32[384]{0:T(512)S(1)} %add_rsqrt_fusion.1, ...), kind=kOutput, calls=%fused_computation.42 | convolution fusion | flops 1891270656 | bytes 13000704 | tf_op jit(solution)/shard_map/dot_general | solution.py:80
  225.9 8.5 %multiply_reduce_fusion.1 = (f32[3,12,128]{2,1,0:T(8,128)S(1)}, f32[3,12,128,512]{3,2,1,0:T(8,128)S(1)}) fusion(f32[3,12,128,512]{3,2,1,0:T(8,128)} %copy-done.1, f32[3,12,128]{2,1,0:T(8,128)S(1)} %log_add_fusion, bf16[3,12,512,64]{2,0,3,1:T(4,128)(2,1)} %copy-done.4, bf16[3,128,12,64]{1,3,2,0:T(8,128)(2,1)} %copy.233, bf16[3]{0:T(256)(128)(2,1)S(1)} %copy-done.59), kind=kOutput, calls=%fused_computation.5 | convolution fusion | flops 311717376 | bytes 21860358 | tf_op jit(solution)/shard_map/spqhd,sphkd->sphqk/dot_general | solution.py:224
  242.3 9.5 %convert_bitcast_fusion.1 = bf16[1,3,512,12,64]{2,1,4,3,0:T(4,128)(2,1)} fusion(f32[3,12,512,64]{2,3,1,0:T(8,128)S(1)} %broadcast_multiply_fusion.1, s32[3,12]{0,1:T(8,128)S(1)} %copy.223), kind=kOutput, calls=%fused_computation.114 | convolution fusion | flops 43647084 | bytes 7078032 | tf_op jit(solution)/shard_map/spht,sphkd->stkhd/dot_general | solution.py:244
  251.8 7.4 %convert_element_type.473 = bf16[1,1536,768]{1,2,0:T(8,128)(2,1)} reshape(bf16[1,3,512,12,64]{2,1,4,3,0:T(4,128)(2,1)} %convert_bitcast_fusion.1) | data formatting | bytes 4718592 | tf_op jit(solution)/shard_map/convert_element_type | solution.py:611
  259.1 13.1 %convert_bitcast_fusion = bf16[1,3,512,12,64]{2,1,4,3,0:T(4,128)(2,1)} fusion(f32[3,12,512,64]{2,3,1,0:T(8,128)} %fusion.220, s32[3,12]{0,1:T(8,128)S(1)} %copy.223), kind=kOutput, calls=%fused_computation.113 | convolution fusion | flops 43647084 | bytes 7078032 | tf_op jit(solution)/shard_map/spht,sphkd->stkhd/dot_general | solution.py:247
  272.2 7.3 %convert_element_type.477 = bf16[1,1536,768]{1,2,0:T(8,128)(2,1)} reshape(bf16[1,3,512,12,64]{2,1,4,3,0:T(4,128)(2,1)} %convert_bitcast_fusion) | data formatting | bytes 4718592 | tf_op jit(solution)/shard_map/convert_element_type | solution.py:611
  279.5 4.9 pad_maximum_fusion
  284.4 12.7 %copy.287 = bf16[2,1536,768]{2,0,1:T(2,128)(2,1)} copy(bf16[2,1536,768]{1,2,0:T(8,128)(2,1)} %pad_maximum_fusion) | data formatting | bytes 9437184
  297.1 5.5 copy.298
  304.0 5.0 convert_reduce_fusion.6
  332.2 24.3 %reduce-scatter.4.cloned.1.call-done = bf16[384,1536]{1,0:T(8,128)(2,1)} async-done(((bf16[1536,1536]{1,0:T(8,128)(2,1)}), bf16[384,1536]{1,0:T(8,128)(2,1)}) %reduce-scatter.4.cloned.1.call-update) | async-done | bytes 1179664
  375.3 6.9 %convert_reduce_fusion.1 = (f32[3072]{0:T(1024)}, bf16[384,3072]{1,0:T(8,128)(2,1)S(1)}) fusion(f32[384,3072]{1,0:T(8,128)} %get-tuple-element.200, f32[3072]{0:T(1024)S(1)} %bitcast.410, bf16[2,3072,768]{2,1,0:T(8,128)(2,1)} %param.36, f32[384,768]{1,0:T(8,128)S(1)} %get-tuple-element.148), kind=kOutput, calls=%fused_computation.73 | convolution fusion | flops 1827566592 | bytes 13000704 | tf_op jit(solution)/shard_map/dot_general | solution.py:90
  391.7 6.9 %multiply_reduce_fusion = (f32[3,12,128]{2,1,0:T(8,128)S(1)}, f32[3,12,128,512]{3,2,1,0:T(8,128)S(1)}) fusion(f32[3,12,128,512]{3,2,1,0:T(8,128)} %copy-done, f32[3,12,128]{2,1,0:T(8,128)S(1)} %copy-done.48, bf16[3,12,512,64]{2,0,3,1:T(4,128)(2,1)} %copy-done.3, bf16[3,128,12,64]{1,3,2,0:T(8,128)(2,1)S(1)} %copy.241, bf16[3]{0:T(256)(128)(2,1)S(1)} %copy-done.59), kind=kOutput, calls=%fused_computation.3 | convolution fusion | flops 311717376 | bytes 21860358 | tf_op jit(solution)/shard_map/spqhd,sphkd->sphqk/dot_general | solution.py:224
  413.6 9.6 %fusion.74 = f32[1,3,512,12,64]{2,1,4,3,0:T(4,128)} fusion(f32[3,12,512,64]{2,3,1,0:T(8,128)S(1)} %broadcast_multiply_fusion, s32[3,12]{0,1:T(8,128)S(1)} %copy-done.53), kind=kOutput, calls=%fused_computation.119 | convolution fusion | flops 42467436 | bytes 9437328 | tf_op jit(solution)/shard_map/spht,sphkd->stkhd/dot_general | solution.py:244
  423.1 8.5 %stack_reshape.20 = f32[1,1,1536,768]{2,3,1,0:T(8,128)} reshape(f32[1,3,512,12,64]{2,1,4,3,0:T(4,128)} %fusion.74) | data formatting | bytes 9437184 | tf_op jit(solution)/shard_map/stack;reshape | solution.py:184
  431.7 13.5 %fusion.77 = f32[1,3,512,12,64]{2,1,4,3,0:T(4,128)} fusion(f32[3,12,512,64]{2,3,1,0:T(8,128)} %fusion.223, s32[3,12]{0,1:T(8,128)S(1)} %copy-done.53), kind=kOutput, calls=%fused_computation.120 | convolution fusion | flops 42467436 | bytes 9437328 | tf_op jit(solution)/shard_map/spht,sphkd->stkhd/dot_general | solution.py:247
  445.2 8.6 %stack_reshape.21 = f32[1,1,1536,768]{2,3,1,0:T(8,128)} reshape(f32[1,3,512,12,64]{2,1,4,3,0:T(4,128)} %fusion.77) | data formatting | bytes 9437184 | tf_op jit(solution)/shard_map/stack;reshape | solution.py:184
  453.8 5.3 fusion.299
  467.4 5.2 pad_maximum_fusion.2.p0
  474.4 61.5 %shard_map.333 = (f32[2,4,6,768]{3,2,1,0:T(8,128)}, f32[24,768]{1,0:T(8,128)}, f32[8,128]{1,0:T(8,128)}) custom-call(bf16[768,3072]{1,0:T(8,128)(2,1)} %pad_maximum_fusion.2.p0, bf16[768,3072]{1,0:T(8,128)(2,1)} %convolution_convert_fusion.1.p1, bf16[3072,768]{1,0:T(8,128)(2,1)} %convolution_convert_fusion.p2, f32[128,128]{1,0:T(8,128)} %concatenate.27.vec), custom_call_target="tpu_custom_call" | custom-call | tf_op jit(solution)/shard_map/pallas_call | solution.py:498
  542.5 6.6 %convolution_convert_fusion.2.p2 = bf16[3072,768]{1,0:T(8,128)(2,1)} fusion(bf16[384,3072]{1,0:T(8,128)(2,1)} %copy-done.117, f32[384,768]{1,0:T(8,128)S(1)} %copy-done.44), kind=kOutput, calls=%fused_computation.35 | convolution fusion | flops 1814593536 | bytes 8257536 | tf_op jit(solution)/shard_map/dot_general | solution.py:84
  560.9 5.5 pad_maximum_fusion.1.p0
  567.2 57.3 %shard_map.332 = (f32[2,4,6,768]{3,2,1,0:T(8,128)}, f32[24,768]{1,0:T(8,128)}, f32[8,128]{1,0:T(8,128)}) custom-call(bf16[768,3072]{1,0:T(8,128)(2,1)} %pad_maximum_fusion.1.p0, bf16[768,3072]{1,0:T(8,128)(2,1)} %convolution_convert_fusion.3.p1, bf16[3072,768]{1,0:T(8,128)(2,1)} %convolution_convert_fusion.2.p2, f32[128,128]{1,0:T(8,128)} %concatenate.25.vec), custom_call_target="tpu_custom_call" | custom-call | tf_op jit(solution)/shard_map/pallas_call | solution.py:498
  (485 shorter events, 225.3 us)
Async XLA Ops:
  7.2 137.6 %all-gather.2.cloned.1.call-start = ((), (), s32[]{:S(2)}) async-start(), calls=%async_computation.1 | async-start | bytes 5898240 | tf_op jit(solution)/shard_map/all_gather | solution.py:49
  10.7 13.2 %copy-start.81 = (bf16[2,768]{1,0:T(2,128)(2,1)S(1)}, bf16[2,768]{1,0:T(2,128)(2,1)}, u32[]{:S(2)}) copy-start(bf16[2,768]{1,0:T(2,128)(2,1)} %param.31) | copy-start | bytes 9220
  10.7 13.8 %copy-start.115 = (s32[12,2]{0,1:T(2,128)S(1)}, s32[12,2]{0,1:T(2,128)}, u32[]{:S(2)}) copy-start(s32[12,2]{0,1:T(2,128)} %param.25) | copy-start | bytes 292
  10.7 13.9 %copy-start.114 = (s32[12,3]{0,1:T(4,128)S(1)}, s32[12,3]{0,1:T(4,128)}, u32[]{:S(2)}) copy-start(s32[12,3]{0,1:T(4,128)} %param.26) | copy-start | bytes 436
  10.7 14.0 %copy-start.18 = (bf16[1,384,768]{2,1,0:T(8,128)(2,1)S(1)}, bf16[1,384,768]{2,1,0:T(8,128)(2,1)}, u32[]{:S(2)}) copy-start(bf16[1,384,768]{2,1,0:T(8,128)(2,1)} %param.21) | copy-start | bytes 1769476
  14.0 19.7 %collective-permute-start = (bf16[2,1,384,768]{3,2,1,0:T(8,128)(2,1)}, bf16[2,1,384,768]{3,2,1,0:T(8,128)(2,1)}, u32[]{:S(2)}, u32[]{:S(2)}) collective-permute-start(bf16[2,1,384,768]{3,2,1,0:T(8,128)(2,1)} %pad_maximum_fusion.4), channel_id=1, source_target_pairs={{0,1},{1,2},{2,3},{4,5},{5,6},{6,7},{8,9},{9,10},{10,11},{12,13},{... | collective-permute-start | bytes 3538952 | tf_op jit(solution)/shard_map/ppermute | solution.py:34
  20.2 19.3 %collective-permute-start.1 = (bf16[2,1,384,768]{3,2,1,0:T(8,128)(2,1)}, bf16[2,1,384,768]{3,2,1,0:T(8,128)(2,1)}, u32[]{:S(2)}, u32[]{:S(2)}) collective-permute-start(bf16[2,1,384,768]{3,2,1,0:T(8,128)(2,1)} %pad_maximum_fusion.4), channel_id=1, source_target_pairs={{1,0},{2,1},{3,2},{5,4},{6,5},{7,6},{9,8},{10,9},{11,10},{13,12},{... | collective-permute-start | bytes 3538952 | tf_op jit(solution)/shard_map/ppermute | solution.py:35
  27.6 42.6 %copy-start.52 = (s32[3,12]{0,1:T(8,128)}, s32[3,12]{0,1:T(8,128)S(1)}, u32[]{:S(2)}) copy-start(s32[3,12]{0,1:T(8,128)S(1)} %copy.214) | copy-start | bytes 436
  70.2 13.2 %slice-start.12 = ((s8[9437184]{0:T(1024)(128)(4,1)}), s8[4194304]{0:T(1024)(128)(4,1)S(1)}, s32[]{:S(2)}) async-start(s8[9437184]{0:T(1024)(128)(4,1)} %bitcast.419), calls=%async_computation.15 | async-start | bytes 8388608
  82.2 15.1 %copy-start.31 = (bf16[1,3,128,12,64]{2,1,4,3,0:T(4,128)(2,1)}, bf16[1,3,128,12,64]{2,1,4,3,0:T(4,128)(2,1)S(1)}, u32[]{:S(2)}) copy-start(bf16[1,3,128,12,64]{2,1,4,3,0:T(4,128)(2,1)S(1)} %copy.221) | copy-start | bytes 1769476
  82.3 15.1 %slice-start.6 = ((s8[9437184]{0:T(1024)(128)(4,1)}), s8[4194304]{0:T(1024)(128)(4,1)S(1)}, s32[]{:S(2)}) async-start(s8[9437184]{0:T(1024)(128)(4,1)} %bitcast.415), calls=%async_computation.9 | async-start | bytes 8388608
  83.1 14.3 %copy-start.25 = (f32[384,768]{1,0:T(8,128)}, f32[384,768]{1,0:T(8,128)S(1)}, u32[]{:S(2)}) copy-start(f32[384,768]{1,0:T(8,128)S(1)} %get-tuple-element.198) | copy-start | bytes 3538948
  83.1 14.3 %copy-start.63 = (f32[384]{0:T(512)}, f32[384]{0:T(512)S(1)}, u32[]{:S(2)}) copy-start(f32[384]{0:T(512)S(1)} %broadcast_multiply_fusion.13) | copy-start | bytes 4612
  83.4 14.0 %copy-start.91 = (f32[384]{0:T(512)}, f32[384]{0:T(512)S(1)}, u32[]{:S(2)}) copy-start(f32[384]{0:T(512)S(1)} %add_rsqrt_fusion.3) | copy-start | bytes 4612
  83.4 13.9 %copy-start.112 = (f32[768]{0:T(1024)S(1)}, f32[768]{0:T(1024)}, u32[]{:S(2)}) copy-start(f32[768]{0:T(1024)} %get-tuple-element.134) | copy-start | bytes 9220
  83.5 13.9 %slice-start.7 = ((s8[9437184]{0:T(1024)(128)(4,1)}), s8[4194304]{0:T(1024)(128)(4,1)S(1)}, s32[]{:S(2)}) async-start(s8[9437184]{0:T(1024)(128)(4,1)} %bitcast.415), calls=%async_computation.10 | async-start | bytes 8388608
  83.5 13.9 %slice-start.8 = ((s8[9437184]{0:T(1024)(128)(4,1)}), s8[1048576]{0:T(1024)(128)(4,1)S(1)}, s32[]{:S(2)}) async-start(s8[9437184]{0:T(1024)(128)(4,1)} %bitcast.415), calls=%async_computation.11 | async-start | bytes 2097152
  99.9 92.6 %copy-start.65 = (f32[384]{0:T(512)}, f32[384]{0:T(512)S(1)}, u32[]{:S(2)}) copy-start(f32[384]{0:T(512)S(1)} %add_rsqrt_fusion.2) | copy-start | bytes 4612
  103.3 253.2 %reduce-scatter.4.cloned.1.call-start = ((), (), s32[]{:S(2)}) async-start(), calls=%async_computation.2 | async-start | bytes 5898240
  107.7 56.5 %copy-start.23 = (bf16[3,128,12,64]{1,3,2,0:T(8,128)(2,1)}, bf16[3,128,12,64]{1,3,2,0:T(8,128)(2,1)S(1)}, u32[]{:S(2)}) copy-start(bf16[3,128,12,64]{1,3,2,0:T(8,128)(2,1)S(1)} %copy.228) | copy-start | bytes 1769476
  192.5 13.3 %slice-start.9 = ((s8[9437184]{0:T(1024)(128)(4,1)}), s8[4194304]{0:T(1024)(128)(4,1)S(1)}, s32[]{:S(2)}) async-start(s8[9437184]{0:T(1024)(128)(4,1)} %bitcast.417), calls=%async_computation.12 | async-start | bytes 8388608
  193.4 25.1 %copy-start.28 = (f32[384,768]{1,0:T(8,128)}, f32[384,768]{1,0:T(8,128)S(1)}, u32[]{:S(2)}) copy-start(f32[384,768]{1,0:T(8,128)S(1)} %get-tuple-element.206) | copy-start | bytes 3538948
  193.4 25.1 %copy-start.67 = (f32[384]{0:T(512)}, f32[384]{0:T(512)S(1)}, u32[]{:S(2)}) copy-start(f32[384]{0:T(512)S(1)} %broadcast_multiply_fusion.11) | copy-start | bytes 4612
  193.7 24.8 %copy-start.94 = (f32[384]{0:T(512)}, f32[384]{0:T(512)S(1)}, u32[]{:S(2)}) copy-start(f32[384]{0:T(512)S(1)} %add_rsqrt_fusion.1) | copy-start | bytes 4612
  193.8 12.1 %copy-start.105 = (f32[768]{0:T(1024)S(1)}, f32[768]{0:T(1024)}, u32[]{:S(2)}) copy-start(f32[768]{0:T(1024)} %get-tuple-element.133) | copy-start | bytes 9220
  193.8 12.1 %slice-start.10 = ((s8[9437184]{0:T(1024)(128)(4,1)}), s8[4194304]{0:T(1024)(128)(4,1)S(1)}, s32[]{:S(2)}) async-start(s8[9437184]{0:T(1024)(128)(4,1)} %bitcast.417), calls=%async_computation.13 | async-start | bytes 8388608
  220.4 14.0 %slice-start.3 = ((s8[9437184]{0:T(1024)(128)(4,1)}), s8[1048576]{0:T(1024)(128)(4,1)S(1)}, s32[]{:S(2)}) async-start(s8[9437184]{0:T(1024)(128)(4,1)} %bitcast.392), calls=%async_computation.6 | async-start | bytes 2097152
  460.8 93.3 %collective-permute-start.2 = (bf16[2,1,384,768]{2,3,1,0:T(8,128)(2,1)}, bf16[2,1,384,768]{2,3,1,0:T(8,128)(2,1)}, u32[]{:S(2)}, u32[]{:S(2)}) collective-permute-start(bf16[2,1,384,768]{2,3,1,0:T(8,128)(2,1)} %get-tuple-element.163), channel_id=1, source_target_pairs={{0,1},{1,2},{2,3},{4,5},{5,6},{6,7},{8,9},{9,10},{10,11},{12,13},{... | collective-permute-start | bytes 3538952 | tf_op jit(solution)/shard_map/ppermute | solution.py:43
  463.3 90.8 %collective-permute-start.3 = (bf16[2,1,384,768]{2,3,1,0:T(8,128)(2,1)}, bf16[2,1,384,768]{2,3,1,0:T(8,128)(2,1)}, u32[]{:S(2)}, u32[]{:S(2)}) collective-permute-start(bf16[2,1,384,768]{2,3,1,0:T(8,128)(2,1)} %get-tuple-element.164), channel_id=1, source_target_pairs={{1,0},{2,1},{3,2},{5,4},{6,5},{7,6},{9,8},{10,9},{11,10},{13,12},{... | collective-permute-start | bytes 3538952 | tf_op jit(solution)/shard_map/ppermute | solution.py:43
  474.4 62.5 %copy-start.40 = (bf16[2,768,768]{2,1,0:T(8,128)(2,1)S(1)}, bf16[2,768,768]{2,1,0:T(8,128)(2,1)}, u32[]{:S(2)}) copy-start(bf16[2,768,768]{2,1,0:T(8,128)(2,1)} %param.27) | copy-start | bytes 7077892
  567.2 63.4 %copy-start.30 = (f32[384,768]{1,0:T(8,128)S(1)}, f32[384,768]{1,0:T(8,128)}, u32[]{:S(2)}) copy-start(f32[384,768]{1,0:T(8,128)} %convolution_add_fusion.2) | copy-start | bytes 3538948
  567.2 63.4 %copy-start.42 = (bf16[2,768,768]{2,1,0:T(8,128)(2,1)S(1)}, bf16[2,768,768]{2,1,0:T(8,128)(2,1)}, u32[]{:S(2)}) copy-start(bf16[2,768,768]{2,1,0:T(8,128)(2,1)} %param.28) | copy-start | bytes 7077892
  (119 other events, 622.6 us)
Sparse Core Ops, SparseCore 0:
  103.4 41.2 all-gather.1
  302.8 53.7 reduce-scatter.3
